TPU v7x, 32 devices: a whole 2x2x4 slice. The times are simulated.
32 devices in a mesh: inner: 4 (over z), outer: 8 (over y, x, core).
Axes of the slice: x: 2, y: 2, z: 4, core: 2. Of those that a mesh axis runs over, the one named last changes fastest.
Arguments:
- features: bfloat16 [262144, 256], P(('inner', 'outer')), may hold values from -6 to 6
- tiles: bfloat16 [2048, 8, 128, 128], P(('inner', 'outer')), may hold values from -0.1875 to 0.1875
- tile_src: int32 [2048, 8], P(('inner', 'outer')), may hold values from 0 to 111, as said below
- tile_count: int32 [2048], P(('inner', 'outer')), may hold values from 1 to 8
- node_count: int32 [32], P(('inner', 'outer')), may hold values from 2730 to 8192
- boundary: int32 [32, 8], P(('inner', 'outer')), may hold values from 0 to 63, as said below
- send_inner: int32 [32, 4, 4], P(('inner', 'outer')), may hold values from 0 to 7
- count_inner: int32 [32, 4], P(('inner', 'outer')), may hold values from 0 to 4, as said below
- send_outer: int32 [32, 8, 4], P(('inner', 'outer')), may hold values from 0 to 7
- count_outer: int32 [32, 8], P(('inner', 'outer')), may hold values from 0 to 4, as said below
- w_first: bfloat16 [256, 256], replicated, may hold values from -0.375 to 0.375
- gamma: float32 [256], replicated, may hold values from 0.25 to 1.75
- beta: float32 [256], replicated, may hold values from -3 to 3
- w_second: bfloat16 [256, 256], replicated, may hold values from -0.375 to 0.375
- b_second: float32 [256], replicated, may hold values from -3 to 3
Outputs:
- updated: bfloat16 [262144, 256], P(('inner', 'outer'))
Inputs may be any that keep to these rules, and one draw needn't show every extreme that they name: `tile_src`: index into the partition's source table; a slot index that is read names a slot its sender fills. `boundary`: distinct block numbers within a partition. `count_inner`: zero toward the partition itself, at least one toward every other peer. `count_outer`: zero toward the partition itself, at least one toward every other peer.
All inputs are finite; a program needn't handle non-finite values.
Results may differ from a plain program's by a relative error of at most 0.0053.
Values may be sent and summed in bfloat16 or wider, within the bound.
A program may use at most 128 MiB of HBM per device.

v0:
```python
import math
import jax
import jax.numpy as jnp
from jax import lax
from jax.sharding import PartitionSpec as P

EPSILON = 1e-05


def packed(blocks, border, lists, counts, capacity):
    chosen = blocks[border[lists]]
    keep = jnp.arange(capacity)[None, :] < counts[:, None]
    return jnp.where(keep[:, :, None, None], chosen, jnp.zeros((), blocks.dtype))


def local(
    features,
    tiles,
    tile_src,
    tile_count,
    node_count,
    boundary,
    send_inner,
    count_inner,
    send_outer,
    count_outer,
    w_first,
    gamma,
    beta,
    w_second,
    b_second,
):
    node_dev, width = features.shape
    nblocks, per_block, block_rows = (tiles.shape[0], tiles.shape[1], tiles.shape[2])
    capacity = send_inner.shape[2]
    zero_bf = jnp.zeros((), jnp.bfloat16)
    filled = node_count[0]
    live = jnp.arange(node_dev) < filled
    features_live = jnp.where(live[:, None], features, zero_bf)
    blocks = features_live.reshape(nblocks, block_rows, width)
    border = boundary[0]
    from_inner = lax.all_to_all(
        packed(blocks, border, send_inner[0], count_inner[0], capacity),
        "inner",
        split_axis=0,
        concat_axis=0,
        tiled=True,
    )
    from_outer = lax.all_to_all(
        packed(blocks, border, send_outer[0], count_outer[0], capacity),
        "outer",
        split_axis=0,
        concat_axis=0,
        tiled=True,
    )
    table = jnp.concatenate(
        [
            blocks,
            from_inner.reshape(-1, block_rows, width),
            from_outer.reshape(-1, block_rows, width),
            jnp.zeros((1, block_rows, width), jnp.bfloat16),
        ],
        axis=0,
    )
    empty_slot = table.shape[0] - 1
    used = jnp.arange(per_block)[None, :] < tile_count[:, None]
    sources = jnp.where(used, tile_src, empty_slot)
    group = math.gcd(nblocks, 8)

    def aggregate(item):
        tile_group, source_group = item
        gathered = table[source_group]
        return jnp.einsum(
            "bjrk,bjkf->brf", tile_group, gathered, preferred_element_type=jnp.float32
        )

    summed = lax.map(
        aggregate,
        (
            tiles.reshape(-1, group, per_block, block_rows, block_rows),
            sources.reshape(-1, group, per_block),
        ),
    )
    combined = (features_live.astype(jnp.float32) + summed.reshape(node_dev, width)).astype(
        jnp.bfloat16
    )
    first = jnp.dot(combined, w_first, preferred_element_type=jnp.float32)
    count_local = filled.astype(jnp.float32).reshape(1)
    masked = jnp.where(live[:, None], first, 0.0)
    totals = lax.psum(
        (count_local, jnp.sum(masked, axis=0), jnp.sum(masked * masked, axis=0)), ("inner", "outer")
    )
    mean = totals[1] / totals[0]
    variance = totals[2] / totals[0] - mean * mean
    normed = jax.nn.relu(gamma * (first - mean) * lax.rsqrt(variance + EPSILON) + beta).astype(
        jnp.bfloat16
    )
    output = jnp.dot(normed, w_second, preferred_element_type=jnp.float32) + b_second
    return jnp.where(live[:, None], output, 0.0).astype(jnp.bfloat16)


def solution(mesh):
    in_specs = (
        P(("inner", "outer"), None),
        P(("inner", "outer"), None, None, None),
        P(("inner", "outer"), None),
        P(("inner", "outer")),
        P(("inner", "outer")),
        P(("inner", "outer"), None),
        P(("inner", "outer"), None, None),
        P(("inner", "outer"), None),
        P(("inner", "outer"), None, None),
        P(("inner", "outer"), None),
        P(),
        P(),
        P(),
        P(),
        P(),
    )
    out_specs = P(("inner", "outer"), None)
    return jax.shard_map(local, mesh=mesh, in_specs=in_specs, out_specs=out_specs, check_vma=False)
```

profile of v0, /device:TPU:12, one launch (start us, length us, event | category | flops | bytes accessed | tf_op | source)
XLA Modules:
  0.0 223.1 jit_solution(13318727625451619962)
XLA Ops:
  1.5 1.3 gather_fusion.1
  3.7 5.2 %broadcast_select_fusion = bf16[8192,256]{1,0:T(8,128)(2,1)} fusion(bf16[8192,256]{1,0:T(8,128)(2,1)} %param.17, pred[8192]{0:T(1024)(128)(4,1)S(1)} %iota_compare_fusion), kind=kLoop, calls=%fused_computation.27 | loop fusion | flops 2097152 | bytes 8396800 | tf_op jit(solution)/shard_map/jit(_where)/select_n | solution.py:39
  9.0 2.8 %gather_fusion.2 = bf16[16,128,256]{2,1,0:T(8,128)(2,1)S(1)} fusion(bf16[64,128,256]{2,1,0:T(8,128)(2,1)} %bitcast.65, s32[1024]{0:T(1024)S(1)} %pad_clamp_fusion.3), kind=kCustom, calls=%fused_computation.2 | custom fusion | bytes 2097216 | tf_op jit(solution)/shard_map/gather | solution.py:11
  11.8 1.1 broadcast_select_fusion.2
  12.9 5.3 %all-to-all-start = ((bf16[4,4,128,256]{3,2,1,0:T(8,128)(2,1)}), bf16[4,4,128,256]{3,2,1,0:T(8,128)(2,1)S(1)}, u32[]{:S(2)}, u32[]{:S(2)}) async-start(bf16[4,4,128,256]{3,2,1,0:T(8,128)(2,1)} %broadcast_select_fusion.2), calls=%async_computation | async-start | bytes 2097152 | tf_op jit(solution)/shard_map/all_to_all | solution.py:42
  19.5 2.9 %gather_fusion.4 = bf16[32,128,256]{2,1,0:T(8,128)(2,1)S(1)} fusion(bf16[64,128,256]{2,1,0:T(8,128)(2,1)} %bitcast.66, s32[1024]{0:T(1024)S(1)} %pad_clamp_fusion.1), kind=kCustom, calls=%fused_computation.4 | custom fusion | bytes 4194432 | tf_op jit(solution)/shard_map/gather | solution.py:11
  22.4 1.6 broadcast_select_fusion.1
  24.0 16.6 %all-to-all-done = bf16[4,4,128,256]{3,2,1,0:T(8,128)(2,1)S(1)} async-done(((bf16[4,4,128,256]{3,2,1,0:T(8,128)(2,1)}), bf16[4,4,128,256]{3,2,1,0:T(8,128)(2,1)S(1)}, u32[]{:S(2)}, u32[]{:S(2)}) %all-to-all-start) | async-done | bytes 1048608 | tf_op jit(solution)/shard_map/all_to_all | solution.py:42
  40.7 4.2 %all-to-all-start.1 = ((bf16[8,4,128,256]{3,2,1,0:T(8,128)(2,1)}), bf16[8,4,128,256]{3,2,1,0:T(8,128)(2,1)S(1)}, u32[]{:S(2)}, u32[]{:S(2)}) async-start(bf16[8,4,128,256]{3,2,1,0:T(8,128)(2,1)} %broadcast_select_fusion.1), calls=%async_computation.1 | async-start | bytes 4194304 | tf_op jit(solution)/shard_map/all_to_all | solution.py:49
  45.1 25.0 %all-to-all-done.1 = bf16[8,4,128,256]{3,2,1,0:T(8,128)(2,1)S(1)} async-done(((bf16[8,4,128,256]{3,2,1,0:T(8,128)(2,1)}), bf16[8,4,128,256]{3,2,1,0:T(8,128)(2,1)S(1)}, u32[]{:S(2)}, u32[]{:S(2)}) %all-to-all-start.1) | async-done | bytes 2097184 | tf_op jit(solution)/shard_map/all_to_all | solution.py:49
  70.1 6.0 %maximum_maximum_fusion = bf16[113,128,256]{2,1,0:T(8,128)(2,1)} fusion(bf16[32,128,256]{2,1,0:T(8,128)(2,1)S(1)} %bitcast.69, bf16[16,128,256]{2,1,0:T(8,128)(2,1)S(1)} %bitcast.71, bf16[64,128,256]{2,1,0:T(8,128)(2,1)} %bitcast.67, bf16[113]{0:T(256)(128)(2,1)S(1)} %pad.3.clone), kind=kLoop, calls=%fused_computation.21 | loop fusion | flops 11108352 | bytes 14745826 | tf_op jit(solution)/shard_map/concatenate | solution.py:56
  76.1 85.3 %while.10 = (s32[]{:T(128)}, f32[8,8,128,256]{3,2,1,0:T(8,128)}, bf16[8,8,8,128,128]{4,3,2,1,0:T(8,128)(2,1)}, s32[8,8,8]{2,1,0:T(8,128)S(1)}, bf16[113,128,256]{2,1,0:T(8,128)(2,1)}, /*index=5*/s32[]{:T(128)}) while((s32[]{:T(128)}, f32[8,8,128,256]{3,2,1,0:T(8,128)}, bf16[8,8,8,128,128]{4,3,2,1,0:T(8,128)(2,1)}, s32[8,8,8]{2,1,0:T(8,128)S(1)}, ...), condition=%wide.region_1.2_spmd, body=%wide.region_0.1_spmd.sunk | while | flops 536872128 | bytes 15735369 | solution.py:77
  76.2 5.9 %gather_fusion = bf16[64,128,256]{2,1,0:T(8,128)(2,1)} fusion(bf16[113,128,256]{2,1,0:T(8,128)(2,1)} %get-tuple-element.98, s32[1024]{0:T(1024)S(1)} %pad_clamp_fusion.6), kind=kCustom, calls=%fused_computation.clone.1 | custom fusion | bytes 8388864 | tf_op jit(solution)/shard_map/while/body/eval_jaxpr/gather | solution.py:72
  82.1 4.6 %fusion.29 = f32[8,8,128,256]{3,2,1,0:T(8,128)} fusion(f32[8,8,128,256]{3,2,1,0:T(8,128)} %get-tuple-element.89, s32[]{:T(128)} %get-tuple-element.88, bf16[8,8,128,256]{3,2,1,0:T(8,128)(2,1)} %bitcast.64, bf16[8,8,8,128,128]{4,3,2,1,0:T(8,128)(2,1)} %get-tuple-element.96), kind=kOutput, calls=%fused_computation.9.clone.1 | convolution fusion | flops 536870912 | bytes 7341056 | tf_op jit(solution)/shard_map/while/body/eval_jaxpr/bjrk,bjkf->brf/dot_general | solution.py:73
  86.8 5.9 %gather_fusion = bf16[64,128,256]{2,1,0:T(8,128)(2,1)} fusion(bf16[113,128,256]{2,1,0:T(8,128)(2,1)} %get-tuple-element.98, s32[1024]{0:T(1024)S(1)} %pad_clamp_fusion.6), kind=kCustom, calls=%fused_computation.clone.1 | custom fusion | bytes 8388864 | tf_op jit(solution)/shard_map/while/body/eval_jaxpr/gather | solution.py:72
  92.8 4.7 %fusion.29 = f32[8,8,128,256]{3,2,1,0:T(8,128)} fusion(f32[8,8,128,256]{3,2,1,0:T(8,128)} %get-tuple-element.89, s32[]{:T(128)} %get-tuple-element.88, bf16[8,8,128,256]{3,2,1,0:T(8,128)(2,1)} %bitcast.64, bf16[8,8,8,128,128]{4,3,2,1,0:T(8,128)(2,1)} %get-tuple-element.96), kind=kOutput, calls=%fused_computation.9.clone.1 | convolution fusion | flops 536870912 | bytes 7341056 | tf_op jit(solution)/shard_map/while/body/eval_jaxpr/bjrk,bjkf->brf/dot_general | solution.py:73
  97.5 5.9 %gather_fusion = bf16[64,128,256]{2,1,0:T(8,128)(2,1)} fusion(bf16[113,128,256]{2,1,0:T(8,128)(2,1)} %get-tuple-element.98, s32[1024]{0:T(1024)S(1)} %pad_clamp_fusion.6), kind=kCustom, calls=%fused_computation.clone.1 | custom fusion | bytes 8388864 | tf_op jit(solution)/shard_map/while/body/eval_jaxpr/gather | solution.py:72
  103.5 4.6 %fusion.29 = f32[8,8,128,256]{3,2,1,0:T(8,128)} fusion(f32[8,8,128,256]{3,2,1,0:T(8,128)} %get-tuple-element.89, s32[]{:T(128)} %get-tuple-element.88, bf16[8,8,128,256]{3,2,1,0:T(8,128)(2,1)} %bitcast.64, bf16[8,8,8,128,128]{4,3,2,1,0:T(8,128)(2,1)} %get-tuple-element.96), kind=kOutput, calls=%fused_computation.9.clone.1 | convolution fusion | flops 536870912 | bytes 7341056 | tf_op jit(solution)/shard_map/while/body/eval_jaxpr/bjrk,bjkf->brf/dot_general | solution.py:73
  108.2 5.9 %gather_fusion = bf16[64,128,256]{2,1,0:T(8,128)(2,1)} fusion(bf16[113,128,256]{2,1,0:T(8,128)(2,1)} %get-tuple-element.98, s32[1024]{0:T(1024)S(1)} %pad_clamp_fusion.6), kind=kCustom, calls=%fused_computation.clone.1 | custom fusion | bytes 8388864 | tf_op jit(solution)/shard_map/while/body/eval_jaxpr/gather | solution.py:72
  114.1 4.6 %fusion.29 = f32[8,8,128,256]{3,2,1,0:T(8,128)} fusion(f32[8,8,128,256]{3,2,1,0:T(8,128)} %get-tuple-element.89, s32[]{:T(128)} %get-tuple-element.88, bf16[8,8,128,256]{3,2,1,0:T(8,128)(2,1)} %bitcast.64, bf16[8,8,8,128,128]{4,3,2,1,0:T(8,128)(2,1)} %get-tuple-element.96), kind=kOutput, calls=%fused_computation.9.clone.1 | convolution fusion | flops 536870912 | bytes 7341056 | tf_op jit(solution)/shard_map/while/body/eval_jaxpr/bjrk,bjkf->brf/dot_general | solution.py:73
  118.9 5.9 %gather_fusion = bf16[64,128,256]{2,1,0:T(8,128)(2,1)} fusion(bf16[113,128,256]{2,1,0:T(8,128)(2,1)} %get-tuple-element.98, s32[1024]{0:T(1024)S(1)} %pad_clamp_fusion.6), kind=kCustom, calls=%fused_computation.clone.1 | custom fusion | bytes 8388864 | tf_op jit(solution)/shard_map/while/body/eval_jaxpr/gather | solution.py:72
  124.8 4.6 %fusion.29 = f32[8,8,128,256]{3,2,1,0:T(8,128)} fusion(f32[8,8,128,256]{3,2,1,0:T(8,128)} %get-tuple-element.89, s32[]{:T(128)} %get-tuple-element.88, bf16[8,8,128,256]{3,2,1,0:T(8,128)(2,1)} %bitcast.64, bf16[8,8,8,128,128]{4,3,2,1,0:T(8,128)(2,1)} %get-tuple-element.96), kind=kOutput, calls=%fused_computation.9.clone.1 | convolution fusion | flops 536870912 | bytes 7341056 | tf_op jit(solution)/shard_map/while/body/eval_jaxpr/bjrk,bjkf->brf/dot_general | solution.py:73
  129.5 5.9 %gather_fusion = bf16[64,128,256]{2,1,0:T(8,128)(2,1)} fusion(bf16[113,128,256]{2,1,0:T(8,128)(2,1)} %get-tuple-element.98, s32[1024]{0:T(1024)S(1)} %pad_clamp_fusion.6), kind=kCustom, calls=%fused_computation.clone.1 | custom fusion | bytes 8388864 | tf_op jit(solution)/shard_map/while/body/eval_jaxpr/gather | solution.py:72
  135.4 4.6 %fusion.29 = f32[8,8,128,256]{3,2,1,0:T(8,128)} fusion(f32[8,8,128,256]{3,2,1,0:T(8,128)} %get-tuple-element.89, s32[]{:T(128)} %get-tuple-element.88, bf16[8,8,128,256]{3,2,1,0:T(8,128)(2,1)} %bitcast.64, bf16[8,8,8,128,128]{4,3,2,1,0:T(8,128)(2,1)} %get-tuple-element.96), kind=kOutput, calls=%fused_computation.9.clone.1 | convolution fusion | flops 536870912 | bytes 7341056 | tf_op jit(solution)/shard_map/while/body/eval_jaxpr/bjrk,bjkf->brf/dot_general | solution.py:73
  140.2 5.9 %gather_fusion = bf16[64,128,256]{2,1,0:T(8,128)(2,1)} fusion(bf16[113,128,256]{2,1,0:T(8,128)(2,1)} %get-tuple-element.98, s32[1024]{0:T(1024)S(1)} %pad_clamp_fusion.6), kind=kCustom, calls=%fused_computation.clone.1 | custom fusion | bytes 8388864 | tf_op jit(solution)/shard_map/while/body/eval_jaxpr/gather | solution.py:72
  146.1 4.6 %fusion.29 = f32[8,8,128,256]{3,2,1,0:T(8,128)} fusion(f32[8,8,128,256]{3,2,1,0:T(8,128)} %get-tuple-element.89, s32[]{:T(128)} %get-tuple-element.88, bf16[8,8,128,256]{3,2,1,0:T(8,128)(2,1)} %bitcast.64, bf16[8,8,8,128,128]{4,3,2,1,0:T(8,128)(2,1)} %get-tuple-element.96), kind=kOutput, calls=%fused_computation.9.clone.1 | convolution fusion | flops 536870912 | bytes 7341056 | tf_op jit(solution)/shard_map/while/body/eval_jaxpr/bjrk,bjkf->brf/dot_general | solution.py:73
  150.8 5.9 %gather_fusion = bf16[64,128,256]{2,1,0:T(8,128)(2,1)} fusion(bf16[113,128,256]{2,1,0:T(8,128)(2,1)} %get-tuple-element.98, s32[1024]{0:T(1024)S(1)} %pad_clamp_fusion.6), kind=kCustom, calls=%fused_computation.clone.1 | custom fusion | bytes 8388864 | tf_op jit(solution)/shard_map/while/body/eval_jaxpr/gather | solution.py:72
  156.8 4.7 %fusion.29 = f32[8,8,128,256]{3,2,1,0:T(8,128)} fusion(f32[8,8,128,256]{3,2,1,0:T(8,128)} %get-tuple-element.89, s32[]{:T(128)} %get-tuple-element.88, bf16[8,8,128,256]{3,2,1,0:T(8,128)(2,1)} %bitcast.64, bf16[8,8,8,128,128]{4,3,2,1,0:T(8,128)(2,1)} %get-tuple-element.96), kind=kOutput, calls=%fused_computation.9.clone.1 | convolution fusion | flops 536870912 | bytes 7341056 | tf_op jit(solution)/shard_map/while/body/eval_jaxpr/bjrk,bjkf->brf/dot_general | solution.py:73
  161.4 5.5 %fusion.12 = bf16[8192,256]{1,0:T(8,128)(2,1)S(1)} fusion(f32[8,8,128,256]{3,2,1,0:T(8,128)} %get-tuple-element.32, bf16[8192,256]{1,0:T(8,128)(2,1)} %param.17, pred[8192]{0:T(1024)(128)(4,1)S(1)} %iota_compare_fusion), kind=kLoop, calls=%fused_computation.17 | loop fusion | flops 8388608 | bytes 16785408 | tf_op jit(solution)/shard_map/convert_element_type | solution.py:84
  167.0 6.5 %multiply_reduce_fusion = (f32[256]{0:T(256)S(1)}, f32[256]{0:T(256)S(1)}, f32[8192,256]{1,0:T(8,128)}) fusion(pred[8192]{0:T(1024)(128)(4,1)S(1)} %iota_compare_fusion, bf16[8192,256]{1,0:T(8,128)(2,1)S(1)} %fusion.12, bf16[256,256]{1,0:T(8,128)(2,1)S(1)} %copy-done), kind=kOutput, calls=%fused_computation.19 | convolution fusion | flops 1082129920 | bytes 12724224 | tf_op jit(solution)/shard_map/dot_general | solution.py:87
  173.5 42.9 %all-reduce = (f32[256]{0:T(256)S(1)}, f32[]{:T(128)}, f32[256]{0:T(256)S(1)}) all-reduce(f32[256]{0:T(256)S(1)} %get-tuple-element.34, f32[]{:T(128)S(6)} %convert_element_type.17, f32[256]{0:T(256)S(1)} %get-tuple-element.33), channel_id=1, replica_groups=mesh['inner'=4,'outer'=8] {'inner','outer'}, use_global_device_ids=true, to_apply=%region_3.4 | all-reduce | flops 513 | bytes 4104 | tf_op jit(solution)/shard_map/psum | solution.py:90
  217.0 6.1 %fusion.11 = bf16[8192,256]{1,0:T(8,128)(2,1)} fusion(bf16[256,256]{1,0:T(8,128)(2,1)S(1)} %copy-done.5, f32[8192,256]{1,0:T(8,128)} %get-tuple-element.50, f32[256]{0:T(256)S(1)} %copy-done.6, f32[256]{0:T(256)S(1)} %copy-done.7, f32[256]{0:T(256)S(1)} %get-tuple-element.48, f32[256]{0:T(256)S(1)} %get-tuple-element.49, f32[256]{0:T(256)S(1)} %copy-done.8, ...), kind=kOutput, calls=%fused_computation.15 | convolution fusion | flops 1092616192 | bytes 12727296 | tf_op jit(solution)/shard_map/dot_general | solution.py:98
  (70 shorter events, 4.6 us)
Async XLA Ops:
  0.0 167.0 %copy-start = (bf16[256,256]{1,0:T(8,128)(2,1)S(1)}, bf16[256,256]{1,0:T(8,128)(2,1)}, u32[]{:S(2)}) copy-start(bf16[256,256]{1,0:T(8,128)(2,1)} %param.27) | copy-start | bytes 393220
  2.8 15.4 %copy-start.3 = (s32[1,8,4]{1,2,0:T(4,128)S(1)}, s32[1,8,4]{1,2,0:T(4,128)}, u32[]{:S(2)}) copy-start(s32[1,8,4]{1,2,0:T(4,128)} %param.25) | copy-start | bytes 388
  2.8 15.6 %copy-start.1 = (s32[1,8]{1,0:T(1,128)S(1)}, s32[1,8]{1,0:T(1,128)}, u32[]{:S(2)}) copy-start(s32[1,8]{1,0:T(1,128)} %param.22) | copy-start | bytes 100
  9.0 13.4 %copy-start.9 = (s32[1,8]{1,0:T(1,128)S(1)}, s32[1,8]{1,0:T(1,128)}, u32[]{:S(2)}) copy-start(s32[1,8]{1,0:T(1,128)} %param.26) | copy-start | bytes 100
  12.9 27.8 %all-to-all-start = ((bf16[4,4,128,256]{3,2,1,0:T(8,128)(2,1)}), bf16[4,4,128,256]{3,2,1,0:T(8,128)(2,1)S(1)}, u32[]{:S(2)}, u32[]{:S(2)}) async-start(bf16[4,4,128,256]{3,2,1,0:T(8,128)(2,1)} %broadcast_select_fusion.2), calls=%async_computation | async-start | bytes 2097152 | tf_op jit(solution)/shard_map/all_to_all | solution.py:42
  18.4 26.5 %copy-start.2 = (s32[64,8]{0,1:T(8,128)S(1)}, s32[64,8]{0,1:T(8,128)}, u32[]{:S(2)}) copy-start(s32[64,8]{0,1:T(8,128)} %param.19) | copy-start | bytes 6148
  18.4 26.5 %copy-start.4 = (s32[64]{0:T(128)S(1)}, s32[64]{0:T(128)}, u32[]{:S(2)}) copy-start(s32[64]{0:T(128)} %param.20) | copy-start | bytes 772
  40.7 29.4 %all-to-all-start.1 = ((bf16[8,4,128,256]{3,2,1,0:T(8,128)(2,1)}), bf16[8,4,128,256]{3,2,1,0:T(8,128)(2,1)S(1)}, u32[]{:S(2)}, u32[]{:S(2)}) async-start(bf16[8,4,128,256]{3,2,1,0:T(8,128)(2,1)} %broadcast_select_fusion.1), calls=%async_computation.1 | async-start | bytes 4194304 | tf_op jit(solution)/shard_map/all_to_all | solution.py:49
  167.0 50.0 %copy-start.5 = (bf16[256,256]{1,0:T(8,128)(2,1)S(1)}, bf16[256,256]{1,0:T(8,128)(2,1)}, u32[]{:S(2)}) copy-start(bf16[256,256]{1,0:T(8,128)(2,1)} %param.30) | copy-start | bytes 393220
  167.0 50.0 %copy-start.6 = (f32[256]{0:T(256)S(1)}, f32[256]{0:T(256)}, u32[]{:S(2)}) copy-start(f32[256]{0:T(256)} %param.31) | copy-start | bytes 3076
  167.0 50.0 %copy-start.7 = (f32[256]{0:T(256)S(1)}, f32[256]{0:T(256)}, u32[]{:S(2)}) copy-start(f32[256]{0:T(256)} %param.29) | copy-start | bytes 3076
  167.0 50.0 %copy-start.8 = (f32[256]{0:T(256)S(1)}, f32[256]{0:T(256)}, u32[]{:S(2)}) copy-start(f32[256]{0:T(256)} %param.28) | copy-start | bytes 3076
where the time goes:
time: 224 us; the launch traced here: 223 us
  local copies, waits for them, and re-layouts  56.8 us (25%)
  matrix products  49.6 us (22%)
  blocking collectives  42.9 us (19%)
  waiting for transfers between devices  41.6 us (19%)
  other arithmetic  21.8 us (10%)
  starting transfers between devices  9.54 us (4%)
    gather x8, local copies, waits for them, and re-layouts, aggregate(): gathered = table[source_group]  47.4 us
    psum x1, blocking collectives, local(): lax.psum((count_local, jnp.sum(masked, axis=0), jnp.sum(masked * masked,...  42.9 us
    dot_general x8, matrix products, aggregate(): jnp.einsum('bjrk,bjkf->brf', tile_group, gathered, preferred_element_type...  37.1 us
    all_to_all x1, waiting for transfers between devices, local(): lax.all_to_all(packed(blocks, border, send_outer[0], count_outer[0], capa...  25 us
    all_to_all x1, waiting for transfers between devices, local(): lax.all_to_all(packed(blocks, border, send_inner[0], count_inner[0], capa...  16.6 us
    gather x7, local copies, waits for them, and re-layouts, packed(): chosen = blocks[border[lists]]  7.94 us
    dot_general x1, matrix products, local(): first = jnp.dot(combined, w_first, preferred_element_type=jnp.float32)  6.45 us
    dot_general x1, matrix products, local(): jnp.dot(normed, w_second, preferred_element_type=jnp.float32) + b_second  6.09 us
  transfers between devices with their start and end apart: 2, of which 2 were waited for; matrix products, arithmetic and copies ran while one was open for 3% of the time, Pallas kernels for 0%

commit v1 on v0

--- a/solution.py
+++ b/solution.py
@@ -88,7 +88,8 @@
     count_local = filled.astype(jnp.float32).reshape(1)
     masked = jnp.where(live[:, None], first, 0.0)
     totals = lax.psum(
-        (count_local, jnp.sum(masked, axis=0), jnp.sum(masked * masked, axis=0)), ("inner", "outer")
+        lax.psum((count_local, jnp.sum(masked, axis=0), jnp.sum(masked * masked, axis=0)), "outer"),
+        "inner",
     )
     mean = totals[1] / totals[0]
     variance = totals[2] / totals[0] - mean * mean

time: 224 us -> 210 us (0.938); the launches traced: 223 us -> 206 us
  blocking collectives: 42.9 us -> 26.2 us
    psum x1, blocking collectives: 42.9 us -> 14 us  [local(): lax.psum((count_local, jnp.sum(masked, axis=0), jnp.sum(masked * masked,...]
    psum x0 -> x1, blocking collectives: none -> 12.2 us  [local(): lax.psum(lax.psum((count_local, jnp.sum(masked, axis=0), jnp.sum(masked *...]
where the time goes in v1:
time: 210 us; the launch traced here: 206 us
  local copies, waits for them, and re-layouts  56.8 us (27%)
  matrix products  49.7 us (24%)
  waiting for transfers between devices  41.6 us (20%)
  blocking collectives  26.2 us (12%)
  other arithmetic  21.7 us (10%)
  starting transfers between devices  9.54 us (5%)
    gather x8, local copies, waits for them, and re-layouts, aggregate(): gathered = table[source_group]  47.4 us
    dot_general x8, matrix products, aggregate(): jnp.einsum('bjrk,bjkf->brf', tile_group, gathered, preferred_element_type...  37.1 us
    all_to_all x1, waiting for transfers between devices, local(): lax.all_to_all(packed(blocks, border, send_outer[0], count_outer[0], capa...  25 us
    all_to_all x1, waiting for transfers between devices, local(): lax.all_to_all(packed(blocks, border, send_inner[0], count_inner[0], capa...  16.7 us
    psum x1, blocking collectives, local(): lax.psum((count_local, jnp.sum(masked, axis=0), jnp.sum(masked * masked,...  14 us
    psum x1, blocking collectives, local(): lax.psum(lax.psum((count_local, jnp.sum(masked, axis=0), jnp.sum(masked *...  12.2 us
    gather x7, local copies, waits for them, and re-layouts, packed(): chosen = blocks[border[lists]]  7.94 us
    dot_general x1, matrix products, local(): first = jnp.dot(combined, w_first, preferred_element_type=jnp.float32)  6.44 us
  transfers between devices with their start and end apart: 2, of which 2 were waited for; matrix products, arithmetic and copies ran while one was open for 3% of the time, Pallas kernels for 0%

profile of v1, /device:TPU:12, one launch (start us, length us, event | category | flops | bytes accessed | tf_op | source)
XLA Modules:
  0.0 206.4 jit_solution(1146683624874542538)
XLA Ops:
  1.5 1.3 gather_fusion.1
  3.7 5.2 %broadcast_select_fusion = bf16[8192,256]{1,0:T(8,128)(2,1)} fusion(bf16[8192,256]{1,0:T(8,128)(2,1)} %param.17, pred[8192]{0:T(1024)(128)(4,1)S(1)} %iota_compare_fusion), kind=kLoop, calls=%fused_computation.27 | loop fusion | flops 2097152 | bytes 8396800 | tf_op jit(solution)/shard_map/jit(_where)/select_n | solution.py:39
  9.0 2.8 %gather_fusion.2 = bf16[16,128,256]{2,1,0:T(8,128)(2,1)S(1)} fusion(bf16[64,128,256]{2,1,0:T(8,128)(2,1)} %bitcast.67, s32[1024]{0:T(1024)S(1)} %pad_clamp_fusion.3), kind=kCustom, calls=%fused_computation.2 | custom fusion | bytes 2097216 | tf_op jit(solution)/shard_map/gather | solution.py:11
  12.9 5.3 %all-to-all-start = ((bf16[4,4,128,256]{3,2,1,0:T(8,128)(2,1)}), bf16[4,4,128,256]{3,2,1,0:T(8,128)(2,1)S(1)}, u32[]{:S(2)}, u32[]{:S(2)}) async-start(bf16[4,4,128,256]{3,2,1,0:T(8,128)(2,1)} %broadcast_select_fusion.2), calls=%async_computation | async-start | bytes 2097152 | tf_op jit(solution)/shard_map/all_to_all | solution.py:42
  19.5 2.9 %gather_fusion.4 = bf16[32,128,256]{2,1,0:T(8,128)(2,1)S(1)} fusion(bf16[64,128,256]{2,1,0:T(8,128)(2,1)} %bitcast.68, s32[1024]{0:T(1024)S(1)} %pad_clamp_fusion.1), kind=kCustom, calls=%fused_computation.4 | custom fusion | bytes 4194432 | tf_op jit(solution)/shard_map/gather | solution.py:11
  22.5 1.6 broadcast_select_fusion.1
  24.0 16.7 %all-to-all-done = bf16[4,4,128,256]{3,2,1,0:T(8,128)(2,1)S(1)} async-done(((bf16[4,4,128,256]{3,2,1,0:T(8,128)(2,1)}), bf16[4,4,128,256]{3,2,1,0:T(8,128)(2,1)S(1)}, u32[]{:S(2)}, u32[]{:S(2)}) %all-to-all-start) | async-done | bytes 1048608 | tf_op jit(solution)/shard_map/all_to_all | solution.py:42
  40.7 4.2 %all-to-all-start.1 = ((bf16[8,4,128,256]{3,2,1,0:T(8,128)(2,1)}), bf16[8,4,128,256]{3,2,1,0:T(8,128)(2,1)S(1)}, u32[]{:S(2)}, u32[]{:S(2)}) async-start(bf16[8,4,128,256]{3,2,1,0:T(8,128)(2,1)} %broadcast_select_fusion.1), calls=%async_computation.1 | async-start | bytes 4194304 | tf_op jit(solution)/shard_map/all_to_all | solution.py:49
  45.1 25.0 %all-to-all-done.1 = bf16[8,4,128,256]{3,2,1,0:T(8,128)(2,1)S(1)} async-done(((bf16[8,4,128,256]{3,2,1,0:T(8,128)(2,1)}), bf16[8,4,128,256]{3,2,1,0:T(8,128)(2,1)S(1)}, u32[]{:S(2)}, u32[]{:S(2)}) %all-to-all-start.1) | async-done | bytes 2097184 | tf_op jit(solution)/shard_map/all_to_all | solution.py:49
  70.1 6.0 %maximum_maximum_fusion = bf16[113,128,256]{2,1,0:T(8,128)(2,1)} fusion(bf16[32,128,256]{2,1,0:T(8,128)(2,1)S(1)} %bitcast.71, bf16[16,128,256]{2,1,0:T(8,128)(2,1)S(1)} %bitcast.73, bf16[64,128,256]{2,1,0:T(8,128)(2,1)} %bitcast.69, bf16[113]{0:T(256)(128)(2,1)S(1)} %pad.3.clone), kind=kLoop, calls=%fused_computation.21 | loop fusion | flops 11108352 | bytes 14745826 | tf_op jit(solution)/shard_map/concatenate | solution.py:56
  76.0 85.3 %while.10 = (s32[]{:T(128)}, f32[8,8,128,256]{3,2,1,0:T(8,128)}, bf16[8,8,8,128,128]{4,3,2,1,0:T(8,128)(2,1)}, s32[8,8,8]{2,1,0:T(8,128)S(1)}, bf16[113,128,256]{2,1,0:T(8,128)(2,1)}, /*index=5*/s32[]{:T(128)}) while((s32[]{:T(128)}, f32[8,8,128,256]{3,2,1,0:T(8,128)}, bf16[8,8,8,128,128]{4,3,2,1,0:T(8,128)(2,1)}, s32[8,8,8]{2,1,0:T(8,128)S(1)}, ...), condition=%wide.region_1.2_spmd, body=%wide.region_0.1_spmd.sunk | while | flops 536872128 | bytes 15735369 | solution.py:77
  76.1 5.9 %gather_fusion = bf16[64,128,256]{2,1,0:T(8,128)(2,1)} fusion(bf16[113,128,256]{2,1,0:T(8,128)(2,1)} %get-tuple-element.101, s32[1024]{0:T(1024)S(1)} %pad_clamp_fusion.6), kind=kCustom, calls=%fused_computation.clone.1 | custom fusion | bytes 8388864 | tf_op jit(solution)/shard_map/while/body/eval_jaxpr/gather | solution.py:72
  82.1 4.6 %fusion.29 = f32[8,8,128,256]{3,2,1,0:T(8,128)} fusion(f32[8,8,128,256]{3,2,1,0:T(8,128)} %get-tuple-element.92, s32[]{:T(128)} %get-tuple-element.91, bf16[8,8,128,256]{3,2,1,0:T(8,128)(2,1)} %bitcast.66, bf16[8,8,8,128,128]{4,3,2,1,0:T(8,128)(2,1)} %get-tuple-element.99), kind=kOutput, calls=%fused_computation.9.clone.1 | convolution fusion | flops 536870912 | bytes 7341056 | tf_op jit(solution)/shard_map/while/body/eval_jaxpr/bjrk,bjkf->brf/dot_general | solution.py:73
  86.8 5.9 %gather_fusion = bf16[64,128,256]{2,1,0:T(8,128)(2,1)} fusion(bf16[113,128,256]{2,1,0:T(8,128)(2,1)} %get-tuple-element.101, s32[1024]{0:T(1024)S(1)} %pad_clamp_fusion.6), kind=kCustom, calls=%fused_computation.clone.1 | custom fusion | bytes 8388864 | tf_op jit(solution)/shard_map/while/body/eval_jaxpr/gather | solution.py:72
  92.7 4.7 %fusion.29 = f32[8,8,128,256]{3,2,1,0:T(8,128)} fusion(f32[8,8,128,256]{3,2,1,0:T(8,128)} %get-tuple-element.92, s32[]{:T(128)} %get-tuple-element.91, bf16[8,8,128,256]{3,2,1,0:T(8,128)(2,1)} %bitcast.66, bf16[8,8,8,128,128]{4,3,2,1,0:T(8,128)(2,1)} %get-tuple-element.99), kind=kOutput, calls=%fused_computation.9.clone.1 | convolution fusion | flops 536870912 | bytes 7341056 | tf_op jit(solution)/shard_map/while/body/eval_jaxpr/bjrk,bjkf->brf/dot_general | solution.py:73
  97.5 5.9 %gather_fusion = bf16[64,128,256]{2,1,0:T(8,128)(2,1)} fusion(bf16[113,128,256]{2,1,0:T(8,128)(2,1)} %get-tuple-element.101, s32[1024]{0:T(1024)S(1)} %pad_clamp_fusion.6), kind=kCustom, calls=%fused_computation.clone.1 | custom fusion | bytes 8388864 | tf_op jit(solution)/shard_map/while/body/eval_jaxpr/gather | solution.py:72
  103.4 4.6 %fusion.29 = f32[8,8,128,256]{3,2,1,0:T(8,128)} fusion(f32[8,8,128,256]{3,2,1,0:T(8,128)} %get-tuple-element.92, s32[]{:T(128)} %get-tuple-element.91, bf16[8,8,128,256]{3,2,1,0:T(8,128)(2,1)} %bitcast.66, bf16[8,8,8,128,128]{4,3,2,1,0:T(8,128)(2,1)} %get-tuple-element.99), kind=kOutput, calls=%fused_computation.9.clone.1 | convolution fusion | flops 536870912 | bytes 7341056 | tf_op jit(solution)/shard_map/while/body/eval_jaxpr/bjrk,bjkf->brf/dot_general | solution.py:73
  108.1 5.9 %gather_fusion = bf16[64,128,256]{2,1,0:T(8,128)(2,1)} fusion(bf16[113,128,256]{2,1,0:T(8,128)(2,1)} %get-tuple-element.101, s32[1024]{0:T(1024)S(1)} %pad_clamp_fusion.6), kind=kCustom, calls=%fused_computation.clone.1 | custom fusion | bytes 8388864 | tf_op jit(solution)/shard_map/while/body/eval_jaxpr/gather | solution.py:72
  114.1 4.6 %fusion.29 = f32[8,8,128,256]{3,2,1,0:T(8,128)} fusion(f32[8,8,128,256]{3,2,1,0:T(8,128)} %get-tuple-element.92, s32[]{:T(128)} %get-tuple-element.91, bf16[8,8,128,256]{3,2,1,0:T(8,128)(2,1)} %bitcast.66, bf16[8,8,8,128,128]{4,3,2,1,0:T(8,128)(2,1)} %get-tuple-element.99), kind=kOutput, calls=%fused_computation.9.clone.1 | convolution fusion | flops 536870912 | bytes 7341056 | tf_op jit(solution)/shard_map/while/body/eval_jaxpr/bjrk,bjkf->brf/dot_general | solution.py:73
  118.8 5.9 %gather_fusion = bf16[64,128,256]{2,1,0:T(8,128)(2,1)} fusion(bf16[113,128,256]{2,1,0:T(8,128)(2,1)} %get-tuple-element.101, s32[1024]{0:T(1024)S(1)} %pad_clamp_fusion.6), kind=kCustom, calls=%fused_computation.clone.1 | custom fusion | bytes 8388864 | tf_op jit(solution)/shard_map/while/body/eval_jaxpr/gather | solution.py:72
  124.7 4.6 %fusion.29 = f32[8,8,128,256]{3,2,1,0:T(8,128)} fusion(f32[8,8,128,256]{3,2,1,0:T(8,128)} %get-tuple-element.92, s32[]{:T(128)} %get-tuple-element.91, bf16[8,8,128,256]{3,2,1,0:T(8,128)(2,1)} %bitcast.66, bf16[8,8,8,128,128]{4,3,2,1,0:T(8,128)(2,1)} %get-tuple-element.99), kind=kOutput, calls=%fused_computation.9.clone.1 | convolution fusion | flops 536870912 | bytes 7341056 | tf_op jit(solution)/shard_map/while/body/eval_jaxpr/bjrk,bjkf->brf/dot_general | solution.py:73
  129.4 5.9 %gather_fusion = bf16[64,128,256]{2,1,0:T(8,128)(2,1)} fusion(bf16[113,128,256]{2,1,0:T(8,128)(2,1)} %get-tuple-element.101, s32[1024]{0:T(1024)S(1)} %pad_clamp_fusion.6), kind=kCustom, calls=%fused_computation.clone.1 | custom fusion | bytes 8388864 | tf_op jit(solution)/shard_map/while/body/eval_jaxpr/gather | solution.py:72
  135.4 4.7 %fusion.29 = f32[8,8,128,256]{3,2,1,0:T(8,128)} fusion(f32[8,8,128,256]{3,2,1,0:T(8,128)} %get-tuple-element.92, s32[]{:T(128)} %get-tuple-element.91, bf16[8,8,128,256]{3,2,1,0:T(8,128)(2,1)} %bitcast.66, bf16[8,8,8,128,128]{4,3,2,1,0:T(8,128)(2,1)} %get-tuple-element.99), kind=kOutput, calls=%fused_computation.9.clone.1 | convolution fusion | flops 536870912 | bytes 7341056 | tf_op jit(solution)/shard_map/while/body/eval_jaxpr/bjrk,bjkf->brf/dot_general | solution.py:73
  140.1 5.9 %gather_fusion = bf16[64,128,256]{2,1,0:T(8,128)(2,1)} fusion(bf16[113,128,256]{2,1,0:T(8,128)(2,1)} %get-tuple-element.101, s32[1024]{0:T(1024)S(1)} %pad_clamp_fusion.6), kind=kCustom, calls=%fused_computation.clone.1 | custom fusion | bytes 8388864 | tf_op jit(solution)/shard_map/while/body/eval_jaxpr/gather | solution.py:72
  146.1 4.6 %fusion.29 = f32[8,8,128,256]{3,2,1,0:T(8,128)} fusion(f32[8,8,128,256]{3,2,1,0:T(8,128)} %get-tuple-element.92, s32[]{:T(128)} %get-tuple-element.91, bf16[8,8,128,256]{3,2,1,0:T(8,128)(2,1)} %bitcast.66, bf16[8,8,8,128,128]{4,3,2,1,0:T(8,128)(2,1)} %get-tuple-element.99), kind=kOutput, calls=%fused_computation.9.clone.1 | convolution fusion | flops 536870912 | bytes 7341056 | tf_op jit(solution)/shard_map/while/body/eval_jaxpr/bjrk,bjkf->brf/dot_general | solution.py:73
  150.8 5.9 %gather_fusion = bf16[64,128,256]{2,1,0:T(8,128)(2,1)} fusion(bf16[113,128,256]{2,1,0:T(8,128)(2,1)} %get-tuple-element.101, s32[1024]{0:T(1024)S(1)} %pad_clamp_fusion.6), kind=kCustom, calls=%fused_computation.clone.1 | custom fusion | bytes 8388864 | tf_op jit(solution)/shard_map/while/body/eval_jaxpr/gather | solution.py:72
  156.7 4.6 %fusion.29 = f32[8,8,128,256]{3,2,1,0:T(8,128)} fusion(f32[8,8,128,256]{3,2,1,0:T(8,128)} %get-tuple-element.92, s32[]{:T(128)} %get-tuple-element.91, bf16[8,8,128,256]{3,2,1,0:T(8,128)(2,1)} %bitcast.66, bf16[8,8,8,128,128]{4,3,2,1,0:T(8,128)(2,1)} %get-tuple-element.99), kind=kOutput, calls=%fused_computation.9.clone.1 | convolution fusion | flops 536870912 | bytes 7341056 | tf_op jit(solution)/shard_map/while/body/eval_jaxpr/bjrk,bjkf->brf/dot_general | solution.py:73
  161.4 5.5 %fusion.12 = bf16[8192,256]{1,0:T(8,128)(2,1)S(1)} fusion(f32[8,8,128,256]{3,2,1,0:T(8,128)} %get-tuple-element.32, bf16[8192,256]{1,0:T(8,128)(2,1)} %param.17, pred[8192]{0:T(1024)(128)(4,1)S(1)} %iota_compare_fusion), kind=kLoop, calls=%fused_computation.17 | loop fusion | flops 8388608 | bytes 16785408 | tf_op jit(solution)/shard_map/convert_element_type | solution.py:84
  167.0 6.4 %multiply_reduce_fusion = (f32[256]{0:T(256)S(1)}, f32[256]{0:T(256)S(1)}, f32[8192,256]{1,0:T(8,128)}) fusion(pred[8192]{0:T(1024)(128)(4,1)S(1)} %iota_compare_fusion, bf16[8192,256]{1,0:T(8,128)(2,1)S(1)} %fusion.12, bf16[256,256]{1,0:T(8,128)(2,1)S(1)} %copy-done), kind=kOutput, calls=%fused_computation.19 | convolution fusion | flops 1082129920 | bytes 12724224 | tf_op jit(solution)/shard_map/dot_general | solution.py:87
  173.4 14.0 %all-reduce = (f32[256]{0:T(256)S(1)}, f32[1]{0:T(128)}, f32[256]{0:T(256)S(1)}) all-reduce(f32[256]{0:T(256)S(1)} %get-tuple-element.34, f32[1]{0:T(128)} %bitcast.20, f32[256]{0:T(256)S(1)} %get-tuple-element.33), channel_id=1, replica_groups=mesh['inner'=4,'outer'=8] {'outer'}, use_global_device_ids=true, to_apply=%region_3.4 | all-reduce | flops 513 | bytes 4104 | tf_op jit(solution)/shard_map/psum | solution.py:91
  187.4 12.2 %all-reduce.1 = (f32[256]{0:T(256)S(1)}, f32[]{:T(128)}, f32[256]{0:T(256)S(1)}) all-reduce(f32[256]{0:T(256)S(1)} %get-tuple-element.45, f32[]{:T(128)} %bitcast.21, f32[256]{0:T(256)S(1)} %get-tuple-element.47), channel_id=1, replica_groups=mesh['inner'=4,'outer'=8] {'inner'}, use_global_device_ids=true, to_apply=%region_4.5 | all-reduce | flops 513 | bytes 4104 | tf_op jit(solution)/shard_map/psum | solution.py:90
  200.3 6.1 %fusion.11 = bf16[8192,256]{1,0:T(8,128)(2,1)} fusion(bf16[256,256]{1,0:T(8,128)(2,1)S(1)} %copy-done.5, f32[8192,256]{1,0:T(8,128)} %get-tuple-element.53, f32[256]{0:T(256)S(1)} %copy-done.6, f32[256]{0:T(256)S(1)} %copy-done.7, f32[256]{0:T(256)S(1)} %get-tuple-element.51, f32[256]{0:T(256)S(1)} %get-tuple-element.52, f32[256]{0:T(256)S(1)} %copy-done.8, ...), kind=kOutput, calls=%fused_computation.15 | convolution fusion | flops 1092616192 | bytes 12727296 | tf_op jit(solution)/shard_map/dot_general | solution.py:99
  (71 shorter events, 5.7 us)
Async XLA Ops:
  0.0 166.9 %copy-start = (bf16[256,256]{1,0:T(8,128)(2,1)S(1)}, bf16[256,256]{1,0:T(8,128)(2,1)}, u32[]{:S(2)}) copy-start(bf16[256,256]{1,0:T(8,128)(2,1)} %param.27) | copy-start | bytes 393220
  2.8 15.4 %copy-start.3 = (s32[1,8,4]{1,2,0:T(4,128)S(1)}, s32[1,8,4]{1,2,0:T(4,128)}, u32[]{:S(2)}) copy-start(s32[1,8,4]{1,2,0:T(4,128)} %param.25) | copy-start | bytes 388
  2.8 15.6 %copy-start.1 = (s32[1,8]{1,0:T(1,128)S(1)}, s32[1,8]{1,0:T(1,128)}, u32[]{:S(2)}) copy-start(s32[1,8]{1,0:T(1,128)} %param.22) | copy-start | bytes 100
  9.0 13.4 %copy-start.9 = (s32[1,8]{1,0:T(1,128)S(1)}, s32[1,8]{1,0:T(1,128)}, u32[]{:S(2)}) copy-start(s32[1,8]{1,0:T(1,128)} %param.26) | copy-start | bytes 100
  12.9 27.8 %all-to-all-start = ((bf16[4,4,128,256]{3,2,1,0:T(8,128)(2,1)}), bf16[4,4,128,256]{3,2,1,0:T(8,128)(2,1)S(1)}, u32[]{:S(2)}, u32[]{:S(2)}) async-start(bf16[4,4,128,256]{3,2,1,0:T(8,128)(2,1)} %broadcast_select_fusion.2), calls=%async_computation | async-start | bytes 2097152 | tf_op jit(solution)/shard_map/all_to_all | solution.py:42
  18.4 26.5 %copy-start.2 = (s32[64,8]{0,1:T(8,128)S(1)}, s32[64,8]{0,1:T(8,128)}, u32[]{:S(2)}) copy-start(s32[64,8]{0,1:T(8,128)} %param.19) | copy-start | bytes 6148
  18.4 26.5 %copy-start.4 = (s32[64]{0:T(128)S(1)}, s32[64]{0:T(128)}, u32[]{:S(2)}) copy-start(s32[64]{0:T(128)} %param.20) | copy-start | bytes 772
  40.7 29.4 %all-to-all-start.1 = ((bf16[8,4,128,256]{3,2,1,0:T(8,128)(2,1)}), bf16[8,4,128,256]{3,2,1,0:T(8,128)(2,1)S(1)}, u32[]{:S(2)}, u32[]{:S(2)}) async-start(bf16[8,4,128,256]{3,2,1,0:T(8,128)(2,1)} %broadcast_select_fusion.1), calls=%async_computation.1 | async-start | bytes 4194304 | tf_op jit(solution)/shard_map/all_to_all | solution.py:49
  166.9 33.4 %copy-start.5 = (bf16[256,256]{1,0:T(8,128)(2,1)S(1)}, bf16[256,256]{1,0:T(8,128)(2,1)}, u32[]{:S(2)}) copy-start(bf16[256,256]{1,0:T(8,128)(2,1)} %param.30) | copy-start | bytes 393220
  167.0 33.4 %copy-start.6 = (f32[256]{0:T(256)S(1)}, f32[256]{0:T(256)}, u32[]{:S(2)}) copy-start(f32[256]{0:T(256)} %param.31) | copy-start | bytes 3076
  167.0 33.4 %copy-start.7 = (f32[256]{0:T(256)S(1)}, f32[256]{0:T(256)}, u32[]{:S(2)}) copy-start(f32[256]{0:T(256)} %param.29) | copy-start | bytes 3076
  167.0 33.4 %copy-start.8 = (f32[256]{0:T(256)S(1)}, f32[256]{0:T(256)}, u32[]{:S(2)}) copy-start(f32[256]{0:T(256)} %param.28) | copy-start | bytes 3076
